TPU v7x, 512 devices: a whole 4x8x8 slice. The times are simulated.
512 devices in a mesh: dp: 64 (over z_hi, y, core), tensor: 8 (over z_lo, x).
Axes of the slice: x: 4, y: 8, z: 8 (z_hi: 4, z_lo: 2; z = z_hi * 2 + z_lo), core: 2. Of those that a mesh axis runs over, the one named last changes fastest.
Arguments:
- tokens: bfloat16 [32768, 8192], P('dp', 'tensor'), may hold values from -6 to 6
- value_weight: bfloat16 [8192, 1024], P('tensor', 'dp'), may hold values from -0.0625 to 0.0625
- adapter_down_weights: bfloat16 [8, 8192, 64], P(None, 'tensor'), may hold values from -0.0625 to 0.0625
- adapter_up_weights: bfloat16 [8, 64, 1024], P(None, None, 'tensor'), may hold values from -0.75 to 0.75
- value_gradient: bfloat16 [32768, 1024], P(('dp', 'tensor')), may hold values from -12 to 12
- block_adapter_index: int32 [256, 1], replicated, may hold values from 0 to 7
- block_live_rows: int32 [256], replicated, may hold values from 1 to 128
Outputs:
- values_out: bfloat16 [32768, 1024], P(('dp', 'tensor'))
- input_gradient: bfloat16 [32768, 8192], P('dp', 'tensor')
- grad_a: float32 [8, 8192, 64], P(None, 'tensor')
- grad_b: float32 [8, 64, 1024], P(None, None, 'tensor')
Inputs may be any that keep to these rules, and one draw needn't show every extreme that they name: `block_adapter_index`: every adapter names at least one block.
All inputs are finite; a program needn't handle non-finite values.
Results may differ from a plain program's by a relative error of at most 0.02.
Values may be sent and summed in bfloat16 or wider, within the bound.
No kernel may reach another device: no remote copies, remote signals or barrier semaphores. Data moves between devices by JAX's collectives and lax.ppermute only.
A program may use at most 64 MiB of HBM per device.

v0:
```python
import jax
import jax.numpy as jnp
from jax import lax
from jax.sharding import PartitionSpec as P

BLK = 128
ADAPTER_SCALE = 2.0


def shards(
    tokens,
    value_weight,
    adapter_down_weights,
    adapter_up_weights,
    value_gradient,
    block_adapter_index,
    block_live_rows,
):
    local_rows = tokens.shape[0]
    tensor_size = lax.axis_size("tensor")
    own_rows = local_rows // tensor_size
    data_index = lax.axis_index("dp")
    tensor_index = lax.axis_index("tensor")
    adapter_count = adapter_down_weights.shape[0]
    local_width = tokens.shape[1]
    rank_columns = adapter_down_weights.shape[2]
    head_columns = adapter_up_weights.shape[2]
    local_blocks = local_rows // BLK
    all_ids = block_adapter_index[:, 0]
    block_indices = lax.dynamic_slice_in_dim(all_ids, data_index * local_blocks, local_blocks)
    block_fill = lax.dynamic_slice_in_dim(block_live_rows, data_index * local_blocks, local_blocks)
    adapter_range = jnp.arange(adapter_count, dtype=jnp.int32)
    block_onehot = (block_indices[:, None] == adapter_range[None, :]).astype(jnp.float32)
    complete_up_weight = lax.all_gather(adapter_up_weights, "tensor", axis=2, tiled=True)
    up_flat = complete_up_weight.reshape(adapter_count * rank_columns, complete_up_weight.shape[2])
    selected_down_weight = adapter_down_weights[block_indices]
    token_block_rows = tokens.reshape(local_blocks, BLK, local_width)
    reduced_part = jnp.einsum(
        "cpe,cev->cpv", token_block_rows, selected_down_weight, preferred_element_type=jnp.float32
    )
    reduced = lax.psum(reduced_part.astype(jnp.bfloat16), "tensor")
    w_full = lax.all_gather(value_weight, "dp", axis=1, tiled=True)
    base_own = lax.psum_scatter(
        jnp.dot(tokens, w_full, preferred_element_type=jnp.float32).astype(jnp.bfloat16),
        "tensor",
        scatter_dimension=0,
        tiled=True,
    ).astype(jnp.float32)
    row_index = tensor_index * own_rows + jnp.arange(own_rows, dtype=jnp.int32)
    row_block = row_index // BLK
    row_ids = block_indices[row_block]
    row_onehot = row_ids[:, None] == adapter_range[None, :]
    reduced_own = lax.dynamic_slice_in_dim(
        reduced.reshape(local_rows, rank_columns), tensor_index * own_rows, own_rows, 0
    )
    spread = (row_onehot[:, :, None].astype(jnp.bfloat16) * reduced_own[:, None, :]).reshape(
        own_rows, adapter_count * rank_columns
    )
    update = jnp.dot(spread, up_flat, preferred_element_type=jnp.float32)
    values_out = (base_own + ADAPTER_SCALE * update).astype(jnp.bfloat16)
    live_rows = row_index % BLK < block_fill[row_block]
    masked = jnp.where(live_rows[:, None], value_gradient, jnp.zeros_like(value_gradient))
    projected = jnp.einsum("kc,mc->km", masked, up_flat, preferred_element_type=jnp.float32)
    grad_low = jnp.sum(
        projected.reshape(own_rows, adapter_count, rank_columns)
        * row_onehot[:, :, None].astype(jnp.float32),
        axis=1,
    ).astype(jnp.bfloat16)
    whole_grad, whole_low = (
        lax.all_gather(masked, "tensor", axis=0, tiled=True),
        lax.all_gather(grad_low, "tensor", axis=0, tiled=True),
    )
    lowrank_block_rows = whole_low.reshape(local_blocks, BLK, rank_columns)
    base_backward = jnp.einsum("kc,dc->kd", whole_grad, w_full, preferred_element_type=jnp.float32)
    adapter_backward = jnp.einsum(
        "sly,say->sla", lowrank_block_rows, selected_down_weight, preferred_element_type=jnp.float32
    ).reshape(local_rows, local_width)
    input_gradient = (base_backward + ADAPTER_SCALE * adapter_backward).astype(jnp.bfloat16)
    down_terms = jnp.einsum(
        "xgj,xgi->xji", token_block_rows, lowrank_block_rows, preferred_element_type=jnp.float32
    )
    down_local = jnp.einsum(
        "ba,bdr->adr", block_onehot, down_terms, precision=lax.Precision.HIGHEST
    )
    grad_cols = lax.dynamic_slice_in_dim(
        whole_grad, tensor_index * head_columns, head_columns, 1
    ).reshape(local_blocks, BLK, head_columns)
    up_terms = jnp.einsum("bkr,bkc->brc", reduced, grad_cols, preferred_element_type=jnp.float32)
    up_local = jnp.einsum("ba,brc->arc", block_onehot, up_terms, precision=lax.Precision.HIGHEST)
    all_onehot = (all_ids[:, None] == adapter_range[None, :]).astype(jnp.float32)
    tallies = jnp.sum(all_onehot * block_live_rows[:, None].astype(jnp.float32), axis=0)
    factor = ADAPTER_SCALE / tallies
    down_sum, up_sum = lax.psum((down_local, up_local), "dp")
    grad_a = down_sum * factor[:, None, None]
    grad_b = up_sum * factor[:, None, None]
    return (values_out, input_gradient, grad_a, grad_b)


def solution(mesh):
    return jax.shard_map(
        shards,
        mesh=mesh,
        in_specs=(
            P("dp", "tensor"),
            P("tensor", "dp"),
            P(None, "tensor", None),
            P(None, None, "tensor"),
            P(("dp", "tensor"), None),
            P(),
            P(),
        ),
        out_specs=(
            P(("dp", "tensor"), None),
            P("dp", "tensor"),
            P(None, "tensor", None),
            P(None, None, "tensor"),
        ),
        check_vma=False,
    )
```

profile of v0, /device:TPU:8, one launch (start us, length us, event | category | flops | bytes accessed | tf_op | source)
XLA Modules:
  0.0 890.9 jit_solution(14993300499443759841)
XLA Ops:
  7.2 0.0 copy-start
  7.2 0.0 all-gather.6.cloned.1.call-start
  7.2 0.7 all-gather.6.cloned.1.call-update
  7.9 0.0 all-gather.8.cloned.1.call-start
  8.0 0.8 dynamic_slice.17
  8.7 0.6 fusion.26
  9.3 2.6 fusion.21
  11.9 1.6 broadcast_select_fusion
  13.6 0.0 all-gather.8.cloned.1.call-update
  13.6 0.0 all-reduce.4.cloned.1.call-start
  13.6 0.7 fusion.25
  14.4 1.8 gather_fusion
  16.2 1.1 fusion.5
  17.3 0.0 all-reduce.4.cloned.1.call-update
  17.3 0.0 all-gather.4.cloned.1.call-start
  17.4 0.5 all-gather.4.cloned.1.call-update
  17.9 0.0 all-reduce.6.cloned.1.call-start
  18.0 0.6 fusion.27
  18.6 2.6 fusion.23
  21.2 36.1 %all-gather.6.cloned.1.call-done = bf16[8,64,1024]{2,1,0:T(8,128)(2,1)} async-done(((bf16[8,64,128]{2,1,0:T(8,128)(2,1)}), bf16[8,64,1024]{2,1,0:T(8,128)(2,1)}) %all-gather.6.cloned.1.call-update) | async-done | bytes 1048592 | tf_op jit(solution)/shard_map/all_gather | solution.py:34
  57.3 1.9 fusion.4
  59.1 28.3 %all_gather.15 = bf16[512,64]{1,0:T(8,128)(2,1)S(1)} all-gather(bf16[64,64]{1,0:T(8,128)(2,1)S(1)} %fusion.4), channel_id=1, replica_groups=mesh['dp'=64,'tensor'=8] {'tensor'}, dimensions={0}, use_global_device_ids=true | all-gather | bytes 73728 | tf_op jit(solution)/shard_map/all_gather | solution.py:71
  87.4 18.4 %all-gather.8.cloned.1.call-done = bf16[512,1024]{1,0:T(8,128)(2,1)} async-done(((bf16[64,1024]{1,0:T(8,128)(2,1)}), bf16[512,1024]{1,0:T(8,128)(2,1)}) %all-gather.8.cloned.1.call-update) | async-done | bytes 1048592 | tf_op jit(solution)/shard_map/all_gather | solution.py:70
  105.7 0.9 constant_dynamic-slice_fusion
  106.7 85.2 %all-reduce.4.cloned.1.call-done = bf16[4,128,64]{1,2,0:T(8,128)(2,1)} async-done(((bf16[4,128,64]{1,2,0:T(8,128)(2,1)}), bf16[4,128,64]{1,2,0:T(8,128)(2,1)}) %all-reduce.4.cloned.1.call-update) | async-done | bytes 65552 | tf_op jit(solution)/shard_map/psum | solution.py:41
  191.8 1.0 fusion.28
  192.8 1.1 fusion.9
  193.9 0.4 convolution_bitcast_fusion
  194.3 3.2 fusion.6
  197.5 0.0 all-reduce.6.cloned.1.call-update
  197.6 0.0 reduce-scatter.2.cloned.1.call-start
  197.6 81.2 %all-gather.4.cloned.1.call-done = bf16[1024,1024]{0,1:T(8,128)(2,1)} async-done(((bf16[1024,16]{0,1:T(8,128)(2,1)}), bf16[1024,1024]{0,1:T(8,128)(2,1)}) %all-gather.4.cloned.1.call-update) | async-done | bytes 2097168 | tf_op jit(solution)/shard_map/all_gather | solution.py:42
  278.9 3.9 convolution_convert_fusion
  282.7 0.0 reduce-scatter.2.cloned.1.call-update
  282.8 0.1 select_reduce_fusion
  282.9 0.1 constant_dynamic-slice_fusion.1
  283.0 0.1 copy.28
  283.1 0.4 convolution_multiply_fusion
  283.5 0.4 copy-done.5
  283.9 0.8 copy-done.8
  284.8 2.2 fusion
  287.0 548.4 %all-reduce.6.cloned.1.call-done = (f32[8,1024,64]{1,0,2:T(8,128)}, f32[8,64,128]{2,0,1:T(8,128)}) async-done(((f32[8,1024,64]{1,0,2:T(8,128)}, f32[8,64,128]{2,0,1:T(8,128)}), (f32[8,1024,64]{1,0,2:T(8,128)}, f32[8,64,128]{2,0,1:T(8,128)})) %all-reduce.6.cloned.1.call-update) | async-done | bytes 2359312 | tf_op jit(solution)/shard_map/psum | solution.py:93
  835.4 1.8 broadcast_multiply_fusion
  837.3 2.5 copy.34
  839.8 0.1 broadcast_multiply_fusion.1
  839.9 0.8 copy.35
  840.7 41.4 %reduce-scatter.2.cloned.1.call-done = bf16[64,1024]{1,0:T(8,128)(2,1)} async-done(((bf16[512,1024]{1,0:T(8,128)(2,1)}), bf16[64,1024]{1,0:T(8,128)(2,1)}) %reduce-scatter.2.cloned.1.call-update) | async-done | bytes 131088 | tf_op jit(solution)/shard_map/reduce_scatter | solution.py:43
  882.1 2.0 fusion.3
  (20 shorter events, 0.1 us)
Async XLA Ops:
  7.2 9.0 %copy-start = (bf16[512,1024]{1,0:T(8,128)(2,1)S(1)}, bf16[512,1024]{1,0:T(8,128)(2,1)}, u32[]{:S(2)}) copy-start(bf16[512,1024]{1,0:T(8,128)(2,1)} %param.7) | copy-start | bytes 3145732
  7.2 50.1 %all-gather.6.cloned.1.call-start = ((), (), s32[]{:S(2)}) async-start(), calls=%async_computation.4 | async-start | bytes 1179648 | tf_op jit(solution)/shard_map/all_gather | solution.py:34
  7.9 97.8 %all-gather.8.cloned.1.call-start = ((), (), s32[]{:S(2)}) async-start(), calls=%async_computation.5 | async-start | bytes 1179648 | tf_op jit(solution)/shard_map/all_gather | solution.py:70
  13.6 43.7 %copy-start.2 = (bf16[64,1024]{1,0:T(8,128)(2,1)S(1)}, bf16[64,1024]{1,0:T(8,128)(2,1)}, u32[]{:S(2)}) copy-start(bf16[64,1024]{1,0:T(8,128)(2,1)} %broadcast_select_fusion) | copy-start | bytes 393220
  13.6 178.2 %all-reduce.4.cloned.1.call-start = ((), (), s32[]{:S(2)}) async-start(), calls=%async_computation.3 | async-start | bytes 131072 | tf_op jit(solution)/shard_map/psum | solution.py:41
  17.3 261.5 %all-gather.4.cloned.1.call-start = ((), (), s32[]{:S(2)}) async-start(), calls=%async_computation.1 | async-start | bytes 2129920 | tf_op jit(solution)/shard_map/all_gather | solution.py:42
  17.9 817.5 %all-reduce.6.cloned.1.call-start = ((), (), s32[]{:S(2)}) async-start(), calls=%async_computation.6 | async-start | bytes 4718592 | tf_op jit(solution)/shard_map/psum | solution.py:93
  197.5 85.2 %copy-start.7 = (s32[256]{0:T(256)S(1)}, s32[256]{0:T(256)}, u32[]{:S(2)}) copy-start(s32[256]{0:T(256)} %param.13) | copy-start | bytes 3076
  197.5 85.2 %copy-start.6 = (s32[256,1]{0,1:T(1,128)S(1)}, s32[256,1]{0,1:T(1,128)}, u32[]{:S(2)}) copy-start(s32[256,1]{0,1:T(1,128)} %param.12) | copy-start | bytes 3076
  197.6 85.4 %copy-start.4 = (bf16[4,128,64]{1,2,0:T(8,128)(2,1)S(1)}, bf16[4,128,64]{1,2,0:T(8,128)(2,1)}, u32[]{:S(2)}) copy-start(bf16[4,128,64]{1,2,0:T(8,128)(2,1)} %all-reduce.4.cloned.1.call-done) | copy-start | bytes 196612
  197.6 684.5 %reduce-scatter.2.cloned.1.call-start = ((), (), s32[]{:S(2)}) async-start(), calls=%async_computation.2 | async-start | bytes 1179648 | tf_op jit(solution)/shard_map/reduce_scatter | solution.py:43
  282.7 1.2 copy-start.5
  283.1 1.7 copy-start.8
  837.3 2.6 copy-start.3
  837.3 44.8 %copy-start.1 = (bf16[8,64,1024]{2,1,0:T(8,128)(2,1)S(1)}, bf16[8,64,1024]{2,1,0:T(8,128)(2,1)}, u32[]{:S(2)}) copy-start(bf16[8,64,1024]{2,1,0:T(8,128)(2,1)} %all-gather.6.cloned.1.call-done) | copy-start | bytes 3145732
Sparse Core Ops, SparseCore 0:
  10.0 47.1 all-gather.5
  59.9 45.7 all-gather.7
  109.2 82.5 all-reduce.3
  195.6 83.2 all-gather.3
  282.5 552.8 all-reduce.5
  838.1 43.9 reduce-scatter.1
where the time goes:
time: 891 us
  waiting for transfers between devices  812 us (91%)
  blocking collectives  28.3 us (3%)
  matrix products  17.1 us (2%)
  between operations  14.3 us (2%)
  other arithmetic  9.62 us (1%)
  local copies, waits for them, and re-layouts  9.44 us (1%)
    psum x1, waiting for transfers between devices, shards(): down_sum, up_sum = lax.psum((down_local, up_local), 'dp')  548 us
    psum x1, waiting for transfers between devices, shards(): reduced = lax.psum(reduced_part.astype(jnp.bfloat16), 'tensor')  85.2 us
    all_gather x1, waiting for transfers between devices, shards(): w_full = lax.all_gather(value_weight, 'dp', axis=1, tiled=True)  81.2 us
    reduce_scatter x1, waiting for transfers between devices, shards(): lax.psum_scatter(jnp.dot(tokens, w_full, preferred_element_type=jnp.float...  41.4 us
    all_gather x1, waiting for transfers between devices, shards(): lax.all_gather(adapter_up_weights, 'tensor', axis=2, tiled=True)  36.1 us
    all_gather x1, blocking collectives, shards(): lax.all_gather(grad_low, 'tensor', axis=0, tiled=True)  28.3 us
    all_gather x1, waiting for transfers between devices, shards(): lax.all_gather(masked, 'tensor', axis=0, tiled=True)  18.4 us
  transfers between devices with their start and end apart: 6, of which 6 were waited for; matrix products, arithmetic and copies ran while one was open for 4% of the time, Pallas kernels for 0%

commit v1 on v0

--- a/solution.py
+++ b/solution.py
@@ -39,7 +39,9 @@
         "cpe,cev->cpv", token_block_rows, selected_down_weight, preferred_element_type=jnp.float32
     )
     reduced = lax.psum(reduced_part.astype(jnp.bfloat16), "tensor")
-    w_full = lax.all_gather(value_weight, "dp", axis=1, tiled=True)
+    w_full = jnp.concatenate(
+        lax.all_to_all(jnp.stack([value_weight] * lax.axis_size("dp")), "dp", 0, 0), axis=1
+    )
     base_own = lax.psum_scatter(
         jnp.dot(tokens, w_full, preferred_element_type=jnp.float32).astype(jnp.bfloat16),
         "tensor",

time: 891 us -> 856 us (0.961)
  waiting for transfers between devices: 812 us -> 759 us
  starting transfers between devices: 0.24 us -> 17.1 us
    all_gather x1 -> x0, waiting for transfers between devices: 81.2 us -> none  [shards(): w_full = lax.all_gather(value_weight, 'dp', axis=1, tiled=True)]
    all_gather x1, waiting for transfers between devices: 18.4 us -> 53.2 us  [shards(): lax.all_gather(masked, 'tensor', axis=0, tiled=True)]
    psum x1, waiting for transfers between devices: 85.2 us -> 57 us  [shards(): reduced = lax.psum(reduced_part.astype(jnp.bfloat16), 'tensor')]
    all_gather x1, waiting for transfers between devices: 36.1 us -> 61.2 us  [shards(): lax.all_gather(adapter_up_weights, 'tensor', axis=2, tiled=True)]
    all_to_all x0 -> x1, starting transfers between devices: none -> 16.9 us  [shards(): lax.all_to_all(jnp.stack([value_weight] * lax.axis_size('dp')), 'dp', 0, 0)]
  transfers between devices with their start and end apart: 6 -> 6, of which waited for: 6 -> 5; matrix products, arithmetic and copies ran while one was open for 4% -> 4% of each run, Pallas kernels for 0% -> 0%
where the time goes in v1:
time: 856 us
  waiting for transfers between devices  759 us (89%)
  blocking collectives  28.2 us (3%)
  matrix products  18.8 us (2%)
  starting transfers between devices  17.1 us (2%)
  between operations  14 us (2%)
  local copies, waits for them, and re-layouts  9.71 us (1%)
  other arithmetic  8.86 us (1%)
    psum x1, waiting for transfers between devices, shards(): down_sum, up_sum = lax.psum((down_local, up_local), 'dp')  546 us
    all_gather x1, waiting for transfers between devices, shards(): lax.all_gather(adapter_up_weights, 'tensor', axis=2, tiled=True)  61.2 us
    psum x1, waiting for transfers between devices, shards(): reduced = lax.psum(reduced_part.astype(jnp.bfloat16), 'tensor')  57 us
    all_gather x1, waiting for transfers between devices, shards(): lax.all_gather(masked, 'tensor', axis=0, tiled=True)  53.2 us
    reduce_scatter x1, waiting for transfers between devices, shards(): lax.psum_scatter(jnp.dot(tokens, w_full, preferred_element_type=jnp.float...  41.4 us
    all_gather x1, blocking collectives, shards(): lax.all_gather(grad_low, 'tensor', axis=0, tiled=True)  28.2 us
  transfers between devices with their start and end apart: 6, of which 5 were waited for; matrix products, arithmetic and copies ran while one was open for 4% of the time, Pallas kernels for 0%

profile of v1, /device:TPU:8, one launch (start us, length us, event | category | flops | bytes accessed | tf_op | source)
XLA Modules:
  0.0 855.8 jit_solution(738483759114783430)
XLA Ops:
  7.2 0.0 copy-start
  7.2 0.0 all-gather.3.cloned.1.call-start
  7.2 0.7 all-gather.3.cloned.1.call-update
  7.9 0.0 all-gather.5.cloned.1.call-start
  8.0 0.8 dynamic_slice.17
  8.7 0.6 fusion.26
  9.3 2.6 fusion.21
  11.9 1.6 broadcast_select_fusion
  13.6 0.0 all-gather.5.cloned.1.call-update
  13.6 2.3 stack.2
  15.9 16.9 %all-to-all-start = ((bf16[64,1024,16]{1,2,0:T(8,128)(2,1)}), bf16[64,1024,16]{1,2,0:T(8,128)(2,1)}, u32[]{:S(2)}, u32[]{:S(2)}) async-start(bf16[64,1024,16]{1,2,0:T(8,128)(2,1)} %stack.2), calls=%async_computation | async-start | bytes 4194304 | tf_op jit(solution)/shard_map/all_to_all | solution.py:43
  32.8 0.0 copy-start.2
  32.9 0.0 all-reduce.4.cloned.1.call-start
  32.9 0.1 fusion.25
  33.0 0.6 gather_fusion
  33.6 1.1 fusion.5
  34.7 0.0 all-reduce.4.cloned.1.call-update
  34.7 0.0 all-reduce.6.cloned.1.call-start
  34.8 0.6 fusion.27
  35.4 2.5 fusion.23
  37.9 61.2 %all-gather.3.cloned.1.call-done = bf16[8,64,1024]{2,1,0:T(8,128)(2,1)} async-done(((bf16[8,64,128]{2,1,0:T(8,128)(2,1)}), bf16[8,64,1024]{2,1,0:T(8,128)(2,1)}) %all-gather.3.cloned.1.call-update) | async-done | bytes 1048592 | tf_op jit(solution)/shard_map/all_gather | solution.py:34
  99.1 1.9 fusion.4
  100.9 53.2 %all-gather.5.cloned.1.call-done = bf16[512,1024]{1,0:T(8,128)(2,1)} async-done(((bf16[64,1024]{1,0:T(8,128)(2,1)}), bf16[512,1024]{1,0:T(8,128)(2,1)}) %all-gather.5.cloned.1.call-update) | async-done | bytes 1048592 | tf_op jit(solution)/shard_map/all_gather | solution.py:72
  154.1 0.9 constant_dynamic-slice_fusion
  155.0 28.2 %all_gather.11 = bf16[512,64]{1,0:T(8,128)(2,1)S(1)} all-gather(bf16[64,64]{1,0:T(8,128)(2,1)S(1)} %fusion.4), channel_id=1, replica_groups=mesh['dp'=64,'tensor'=8] {'tensor'}, dimensions={0}, use_global_device_ids=true | all-gather | bytes 73728 | tf_op jit(solution)/shard_map/all_gather | solution.py:73
  183.2 57.0 %all-reduce.4.cloned.1.call-done = bf16[4,128,64]{1,2,0:T(8,128)(2,1)} async-done(((bf16[4,128,64]{1,2,0:T(8,128)(2,1)}), bf16[4,128,64]{1,2,0:T(8,128)(2,1)}) %all-reduce.4.cloned.1.call-update) | async-done | bytes 65552 | tf_op jit(solution)/shard_map/psum | solution.py:41
  240.2 1.0 fusion.28
  241.2 1.1 fusion.9
  242.3 0.4 convolution_bitcast_fusion
  242.7 3.2 fusion.6
  245.9 0.0 all-reduce.6.cloned.1.call-update
  246.0 0.0 reduce-scatter.2.cloned.1.call-start
  246.0 0.0 copy-start.8
  246.0 4.0 convolution_convert_fusion
  250.0 0.0 reduce-scatter.2.cloned.1.call-update
  250.0 0.1 select_reduce_fusion
  250.2 0.1 constant_dynamic-slice_fusion.1
  250.3 0.1 copy.29
  250.4 0.4 convolution_multiply_fusion
  250.8 0.4 copy-done.6
  251.2 3.8 fusion
  255.0 545.5 %all-reduce.6.cloned.1.call-done = (f32[8,1024,64]{1,0,2:T(8,128)}, f32[8,64,128]{2,0,1:T(8,128)}) async-done(((f32[8,1024,64]{1,0,2:T(8,128)}, f32[8,64,128]{2,0,1:T(8,128)}), (f32[8,1024,64]{1,0,2:T(8,128)}, f32[8,64,128]{2,0,1:T(8,128)})) %all-reduce.6.cloned.1.call-update) | async-done | bytes 2359312 | tf_op jit(solution)/shard_map/psum | solution.py:95
  800.6 1.8 broadcast_multiply_fusion
  802.5 2.5 copy.35
  805.0 0.1 broadcast_multiply_fusion.1
  805.1 0.8 copy.36
  805.8 41.4 %reduce-scatter.2.cloned.1.call-done = bf16[64,1024]{1,0:T(8,128)(2,1)} async-done(((bf16[512,1024]{1,0:T(8,128)(2,1)}), bf16[64,1024]{1,0:T(8,128)(2,1)}) %reduce-scatter.2.cloned.1.call-update) | async-done | bytes 131088 | tf_op jit(solution)/shard_map/reduce_scatter | solution.py:45
  847.3 2.0 fusion.3
  (20 shorter events, 0.1 us)
Async XLA Ops:
  7.2 26.4 %copy-start = (bf16[512,1024]{1,0:T(8,128)(2,1)S(1)}, bf16[512,1024]{1,0:T(8,128)(2,1)}, u32[]{:S(2)}) copy-start(bf16[512,1024]{1,0:T(8,128)(2,1)} %param.7) | copy-start | bytes 3145732
  7.2 91.9 %all-gather.3.cloned.1.call-start = ((), (), s32[]{:S(2)}) async-start(), calls=%async_computation.4 | async-start | bytes 1179648 | tf_op jit(solution)/shard_map/all_gather | solution.py:34
  7.9 146.2 %all-gather.5.cloned.1.call-start = ((), (), s32[]{:S(2)}) async-start(), calls=%async_computation.5 | async-start | bytes 1179648 | tf_op jit(solution)/shard_map/all_gather | solution.py:72
  15.9 17.0 %copy-start.7 = (s32[256,1]{0,1:T(1,128)S(1)}, s32[256,1]{0,1:T(1,128)}, u32[]{:S(2)}) copy-start(s32[256,1]{0,1:T(1,128)} %param.12) | copy-start | bytes 3076
  15.9 17.1 %copy-start.3 = (bf16[8,1024,64]{1,2,0:T(8,128)(2,1)S(1)}, bf16[8,1024,64]{1,2,0:T(8,128)(2,1)}, u32[]{:S(2)}) copy-start(bf16[8,1024,64]{1,2,0:T(8,128)(2,1)} %param.9) | copy-start | bytes 3145732
  15.9 230.1 %all-to-all-start = ((bf16[64,1024,16]{1,2,0:T(8,128)(2,1)}), bf16[64,1024,16]{1,2,0:T(8,128)(2,1)}, u32[]{:S(2)}, u32[]{:S(2)}) async-start(bf16[64,1024,16]{1,2,0:T(8,128)(2,1)} %stack.2), calls=%async_computation | async-start | bytes 4194304 | tf_op jit(solution)/shard_map/all_to_all | solution.py:43
  32.8 66.2 %copy-start.2 = (bf16[64,1024]{1,0:T(8,128)(2,1)S(1)}, bf16[64,1024]{1,0:T(8,128)(2,1)}, u32[]{:S(2)}) copy-start(bf16[64,1024]{1,0:T(8,128)(2,1)} %broadcast_select_fusion) | copy-start | bytes 393220
  32.9 207.4 %all-reduce.4.cloned.1.call-start = ((), (), s32[]{:S(2)}) async-start(), calls=%async_computation.3 | async-start | bytes 131072 | tf_op jit(solution)/shard_map/psum | solution.py:41
  34.7 765.8 %all-reduce.6.cloned.1.call-start = ((), (), s32[]{:S(2)}) async-start(), calls=%async_computation.6 | async-start | bytes 4718592 | tf_op jit(solution)/shard_map/psum | solution.py:95
  246.0 601.3 %reduce-scatter.2.cloned.1.call-start = ((), (), s32[]{:S(2)}) async-start(), calls=%async_computation.2 | async-start | bytes 1179648 | tf_op jit(solution)/shard_map/reduce_scatter | solution.py:45
  246.0 4.0 copy-start.8
  246.0 4.1 copy-start.5
  250.0 1.2 copy-start.6
  802.4 2.6 copy-start.4
  802.4 44.8 %copy-start.1 = (bf16[8,64,1024]{2,1,0:T(8,128)(2,1)S(1)}, bf16[8,64,1024]{2,1,0:T(8,128)(2,1)}, u32[]{:S(2)}) copy-start(bf16[8,64,1024]{2,1,0:T(8,128)(2,1)} %all-gather.3.cloned.1.call-done) | copy-start | bytes 3145732
Sparse Core Ops, SparseCore 0:
  10.0 89.0 all-gather.2
  101.7 52.3 all-gather.4
  157.6 82.5 all-reduce.3
  246.1 554.4 all-reduce.5
  803.2 43.9 reduce-scatter.1
